TPU v7x, 128 devices: a whole 4x4x4 slice. The times are simulated.
128 devices in a mesh: row: 8 (over x, y_lo), col: 16 (over y_hi, z, core).
Axes of the slice: x: 4, y: 4 (y_hi: 2, y_lo: 2; y = y_hi * 2 + y_lo), z: 4, core: 2. Of those that a mesh axis runs over, the one named last changes fastest.
Arguments:
- front: float32 [10240, 10240], P('row', 'col'), as said below
- updates: float32 [16384, 8192], P('row', 'col'), as said below
- maps: int32 [2, 64], replicated, may hold values from 0 to 79, as said below
Outputs:
- panel_factor: float32 [10240, 2048], P('row', 'col')
- trailing: float32 [10240, 10240], P('row', 'col')
Inputs may be any that keep to these rules, and one draw needn't show every extreme that they name: `maps`: each row lists 64 distinct front blocks; entry j leaves remainder floor(j / 4) on division by 16, the entries of one remainder rise with j, and blocks 0 and 79 appear in both rows. Symmetric in front order; the assembled leading 2048 x 2048 block is positive definite. `updates`: each child's update is symmetric in the child's own order.
All inputs are finite; a program needn't handle non-finite values.
Results may differ from a plain program's by a relative error of at most 0.0001.
Values sent between devices are 32-bit elements; how exact they have to be, the bound alone decides.
No kernel may reach another device: no remote copies, remote signals or barrier semaphores. Data moves between devices by JAX's collectives and lax.ppermute only.
A program may use at most 192 MiB of HBM per device.

v0:
```python
import jax
import jax.numpy as jnp
from jax import lax
from jax.sharding import PartitionSpec as P

BLK = 128
PW = 2048


def from_root(value, axis, source):
    kept = jnp.where(lax.axis_index(axis) == source, value, 0).astype(value.dtype)
    return lax.psum(kept, axis)


def block_cholesky(leading):
    order = leading.shape[0]
    count = order // BLK
    identity = jnp.eye(BLK, dtype=jnp.float32)
    factor = jnp.zeros((order, order), jnp.float32)
    inverses = []
    for step in range(count):
        start = step * BLK
        column = leading[start:, start : start + BLK]
        if step > 0:
            column = column - jnp.dot(
                factor[start:, :start],
                factor[start : start + BLK, :start].T,
                precision=lax.Precision.HIGHEST,
                preferred_element_type=jnp.float32,
            )
        diag_factor = jnp.linalg.cholesky(column[:BLK])
        inverse = jax.scipy.linalg.solve_triangular(diag_factor, identity, lower=True)
        inverses.append(inverse)
        factor = factor.at[start : start + BLK, start : start + BLK].set(diag_factor)
        if start + BLK < order:
            below = jnp.dot(
                column[BLK:],
                inverse.T,
                precision=lax.Precision.HIGHEST,
                preferred_element_type=jnp.float32,
            )
            factor = factor.at[start + BLK :, start : start + BLK].set(below)
    return (factor, inverses)


def block_solve(factor, inverses, rows_in):
    count = len(inverses)
    result = jnp.zeros(rows_in.shape, jnp.float32)
    for step in range(count):
        start = step * BLK
        target = rows_in[:, start : start + BLK]
        if step > 0:
            target = target - jnp.dot(
                result[:, :start],
                factor[start : start + BLK, :start].T,
                precision=lax.Precision.HIGHEST,
                preferred_element_type=jnp.float32,
            )
        solved = jnp.dot(
            target,
            inverses[step].T,
            precision=lax.Precision.HIGHEST,
            preferred_element_type=jnp.float32,
        )
        result = result.at[:, start : start + BLK].set(solved)
    return result


def local(front, updates, maps):
    rows_n = lax.axis_size("row")
    cols_n = lax.axis_size("col")
    half_rows = rows_n // 2
    row_at = lax.axis_index("row")
    col_at = lax.axis_index("col")
    front_rows, front_cols = front.shape
    row_slots = front_rows // BLK
    col_slots = front_cols // BLK
    col_group = updates.shape[1] // BLK
    depth_slots = col_group // half_rows
    width_slots = cols_n // rows_n
    child_blocks = maps.shape[1]
    outgoing = updates.reshape(width_slots, rows_n, depth_slots * BLK, col_group * BLK)
    incoming = lax.all_to_all(outgoing, "row", split_axis=1, concat_axis=1, tiled=True)
    incoming = incoming.reshape(width_slots, 2, half_rows, depth_slots, BLK, col_group, BLK)
    shape_grid = (width_slots, half_rows, depth_slots)
    grid_w = lax.broadcasted_iota(jnp.int32, shape_grid, 0)
    grid_a = lax.broadcasted_iota(jnp.int32, shape_grid, 1)
    grid_e = lax.broadcasted_iota(jnp.int32, shape_grid, 2)
    block_id = (((grid_w * rows_n + row_at) * depth_slots + grid_e) * half_rows + grid_a).reshape(
        -1
    )
    child_iota = jnp.arange(child_blocks, dtype=jnp.int32)
    assembled = front
    for which_child in range(2):
        child_map = maps[which_child]
        blocks = incoming[:, which_child].reshape(
            width_slots * half_rows * depth_slots, BLK, col_group, BLK
        )
        matched = block_id[:, None] == child_iota[None, :]
        targets = jnp.sum(jnp.where(matched, child_map[None, :], 0), axis=1)
        row_place = (
            targets[None, :] // rows_n == jnp.arange(row_slots, dtype=jnp.int32)[:, None]
        ).astype(jnp.float32)
        col_ids = lax.dynamic_slice_in_dim(child_map, col_at * col_group, col_group)
        col_place = (
            col_ids[None, :] // cols_n == jnp.arange(col_slots, dtype=jnp.int32)[:, None]
        ).astype(jnp.float32)
        placed = jnp.einsum("pn,nxvy->pxvy", row_place, blocks, precision=lax.Precision.HIGHEST)
        placed = jnp.einsum("pxvy,qv->pxqy", placed, col_place, precision=lax.Precision.HIGHEST)
        assembled = assembled + placed.reshape(front_rows, front_cols)
    panel_rslots = PW // BLK // rows_n
    panel_cslots = PW // BLK // cols_n
    gathered = lax.all_gather(assembled[:, : panel_cslots * BLK], "col", axis=1, tiled=True)
    panel_rows = (
        gathered.reshape(front_rows, cols_n, panel_cslots, BLK)
        .transpose(0, 2, 1, 3)
        .reshape(front_rows, PW)
    )
    corner = assembled[: panel_rslots * BLK, : panel_cslots * BLK]
    pieces = lax.all_gather(corner, ("row", "col"), axis=0, tiled=True)
    leading = (
        pieces.reshape(rows_n, cols_n, panel_rslots, BLK, panel_cslots, BLK)
        .transpose(2, 0, 3, 4, 1, 5)
        .reshape(PW, PW)
    )
    factor, inverses = block_cholesky(leading)
    lower_rows = block_solve(factor, inverses, panel_rows[panel_rslots * BLK :])
    head_rows = lax.dynamic_index_in_dim(
        factor.reshape(panel_rslots, rows_n, BLK, PW), row_at, 1, keepdims=False
    )
    factor_rows = jnp.concatenate([head_rows.reshape(panel_rslots * BLK, PW), lower_rows], axis=0)
    col_span = cols_n // rows_n
    root_row = col_at % rows_n
    picked = lax.dynamic_index_in_dim(
        factor_rows.reshape(col_slots, col_span, BLK, PW), col_at // rows_n, 1, keepdims=False
    )
    column_rows = from_root(picked.reshape(col_slots * BLK, PW), "row", root_row)
    update = jnp.dot(
        factor_rows,
        column_rows.T,
        precision=lax.Precision.HIGHEST,
        preferred_element_type=jnp.float32,
    )
    row_keep = jnp.arange(front_rows) // BLK >= panel_rslots
    col_keep = jnp.arange(front_cols) // BLK >= panel_cslots
    trailing = jnp.where(
        row_keep[:, None] & col_keep[None, :], assembled - update, jnp.float32(0.0)
    )
    panel_out = lax.dynamic_index_in_dim(
        factor_rows.reshape(front_rows, panel_cslots, cols_n, BLK), col_at, 2, keepdims=False
    )
    return (panel_out.reshape(front_rows, panel_cslots * BLK), trailing)


def solution(mesh):
    in_specs = (P("row", "col"), P("row", "col"), P())
    out_specs = (P("row", "col"), P("row", "col"))
    return jax.shard_map(local, mesh=mesh, in_specs=in_specs, out_specs=out_specs, check_vma=False)
```

profile of v0, /device:TPU:1, one launch (start us, length us, event | category | flops | bytes accessed | tf_op | source)
XLA Modules:
  0.0 1348.0 jit_solution(4815525074434272048)
XLA Ops:
  18.3 58.4 %all-to-all-done = f32[2,8,128,512]{3,2,0,1:T(8,128)} async-done(((f32[2,8,128,512]{3,2,0,1:T(8,128)}), f32[2,8,128,512]{3,2,0,1:T(8,128)}, u32[]{:S(2)}, u32[]{:S(2)}) %all-to-all-start) | async-done | bytes 4194336 | tf_op jit(solution)/shard_map/all_to_all | solution.py:83
  108.5 208.8 %all-gather.3.cloned.1.call-done = f32[32768,128]{1,0:T(8,128)} async-done(((f32[256,128]{1,0:T(8,128)}), f32[32768,128]{1,0:T(8,128)}) %all-gather.3.cloned.1.call-update) | async-done | bytes 16777232 | tf_op jit(solution)/shard_map/all_gather | solution.py:120
  317.3 17.8 %copy.161 = f32[8,16,2,128,1,128]{3,0,2,5,1,4:T(8,128)} copy(f32[8,16,2,128,1,128]{5,3,2,1,0,4:T(8,128)} %bitcast.269) | data formatting | bytes 33554432 | tf_op jit(solution)/shard_map/reshape | solution.py:122
  335.1 18.0 %reshape.1456 = f32[2048,2048]{0,1:T(8,128)} reshape(f32[2,8,128,1,16,128]{2,1,0,5,4,3:T(8,128)} %bitcast.263) | data formatting | bytes 33554432 | tf_op jit(solution)/shard_map/reshape | solution.py:124
  354.9 11.7 cholesky.254
  368.0 9.8 custom-call.20
  392.2 11.9 cholesky.265
  406.1 9.8 custom-call.21
  422.7 11.7 cholesky.276
  436.4 10.0 custom-call.22
  454.1 11.7 cholesky.287
  467.8 9.8 custom-call.23
  486.3 11.7 cholesky.298
  500.0 9.8 custom-call.24
  518.4 11.7 cholesky.309
  532.2 9.8 custom-call.25
  551.2 11.7 cholesky.320
  564.9 9.8 custom-call.26
  583.7 12.1 cholesky.331
  597.8 9.8 custom-call.27
  616.8 11.9 cholesky.342
  630.6 9.8 custom-call.28
  648.9 11.9 cholesky.353
  662.8 9.8 custom-call.29
  681.0 11.7 cholesky.364
  694.7 10.2 custom-call.30
  712.6 11.7 cholesky.375
  726.3 9.8 custom-call.31
  743.5 11.7 cholesky.386
  757.2 9.8 custom-call.32
  773.1 11.9 cholesky.397
  787.0 9.8 custom-call.33
  802.0 11.7 cholesky.408
  815.7 10.2 custom-call.34
  829.8 11.7 cholesky.419
  850.1 9.8 custom-call.35
  922.8 8.5 fusion.87
  934.4 9.7 fusion.119
  947.1 10.5 fusion.96
  960.8 11.5 fusion.122
  975.4 12.6 fusion.72
  991.0 13.4 fusion.75
  1007.5 14.3 %fusion.125 = f32[1024,128]{1,0:T(8,128)S(1)} fusion(f32[1024,2048]{0,1:T(8,128)} %fusion.100, f32[2048,2048]{1,0:T(8,128)} %get-tuple-element.575, f32[1280,2048]{1,0:T(8,128)S(1)} %bitcast.274), kind=kOutput, calls=%fused_computation.126 | convolution fusion | flops 2818703360 | bytes 9306112 | tf_op jit(solution)/shard_map/dot_general | solution.py:53
  1023.3 14.4 %fusion.78 = f32[1024,128]{1,0:T(8,128)S(1)} fusion(f32[1024,2048]{0,1:T(8,128)S(1)} %fusion.99, f32[2048,2048]{1,0:T(8,128)} %get-tuple-element.575, f32[1280,2048]{1,0:T(8,128)S(1)} %bitcast.274), kind=kOutput, calls=%fused_computation.84 | convolution fusion | flops 3020029952 | bytes 9895936 | tf_op jit(solution)/shard_map/dot_general | solution.py:53
  1048.1 13.3 reshape.1460
  1061.3 21.0 %fusion.10 = f32[5,128,2048]{1,0,2:T(8,128)} fusion(pred[]{:T(512)S(6)} %eq.132, f32[5,2,128,2048]{2,1,0,3:T(2,128)} %reshape.1460, s32[]{:T(128)S(6)} %select_n.110), kind=kLoop, calls=%fused_computation.14 | loop fusion | flops 1310720 | bytes 10485765 | tf_op jit(solution)/shard_map/jit(_where)/select_n | solution.py:11
  1098.3 211.5 %all-reduce.4.cloned.1.call-done = f32[640,2048]{0,1:T(8,128)} async-done(((f32[640,2048]{0,1:T(8,128)}), f32[640,2048]{0,1:T(8,128)}) %all-reduce.4.cloned.1.call-update) | async-done | bytes 5242896 | tf_op jit(solution)/shard_map/psum | solution.py:12
  1309.8 31.6 %fusion.33 = f32[1280,640]{1,0:T(8,128)} fusion(f32[1280,640]{1,0:T(8,128)} %copy-done.5, f32[640,2048]{0,1:T(8,128)} %all-reduce.4.cloned.1.call-done, pred[640]{0:T(1024)(128)(4,1)S(1)} %fusion.278, pred[1280]{0:T(1024)(128)(4,1)S(1)} %fusion.274, f32[1024,2048]{0,1:T(8,128)} %copy-done.1, f32[256,2048]{0,1:T(8,128)S(1)} %copy-done.4), kind=kOutput, calls=%fused_computation.39 | convolution fusion | flops 20137738240 | bytes 22284160 | tf_op jit(solution)/shard_map/dot_general | solution.py:138
  (236 shorter events, 311.6 us)
Async XLA Ops:
  7.2 10.9 copy-start.8
  11.9 64.8 %all-to-all-start = ((f32[2,8,128,512]{3,2,0,1:T(8,128)}), f32[2,8,128,512]{3,2,0,1:T(8,128)}, u32[]{:S(2)}, u32[]{:S(2)}) async-start(f32[2,8,128,512]{3,2,0,1:T(8,128)} %copy.156), calls=%async_computation | async-start | bytes 8388608 | tf_op jit(solution)/shard_map/all_to_all | solution.py:83
  17.8 299.5 %all-gather.3.cloned.1.call-start = ((), (), s32[]{:S(2)}) async-start(), calls=%async_computation.1 | async-start | bytes 16908288 | tf_op jit(solution)/shard_map/all_gather | solution.py:120
  89.3 9.9 copy-start.6
  101.1 234.0 %copy-start.5 = (f32[1280,640]{1,0:T(8,128)}, f32[1280,640]{1,0:T(8,128)S(1)}, u32[]{:S(2)}) copy-start(f32[1280,640]{1,0:T(8,128)S(1)} %bitcast_add_fusion) | copy-start | bytes 9830404
  101.8 741.7 %all-gather.5.cloned.1.call-start = ((), (), s32[]{:S(2)}) async-start(), calls=%async_computation.2 | async-start | bytes 11141120 | tf_op jit(solution)/shard_map/all_gather | solution.py:113
  108.5 1201.3 %all-reduce.4.cloned.1.call-start = ((), (), s32[]{:S(2)}) async-start(), calls=%async_computation.3 | async-start | bytes 10485760 | tf_op jit(solution)/shard_map/psum | solution.py:12
  862.6 35.1 %copy-start.2 = (f32[2,1,128,2048]{3,2,1,0:T(8,128)}, f32[2,1,128,2048]{3,2,1,0:T(8,128)S(1)}, u32[]{:S(2)}) copy-start(f32[2,1,128,2048]{3,2,1,0:T(8,128)S(1)} %constant_dynamic-slice_fusion) | copy-start | bytes 6291460
  875.3 35.9 %slice-start = ((s8[10485760]{0:T(1024)(128)(4,1)}), s8[4194304]{0:T(1024)(128)(4,1)S(1)}, s32[]{:S(2)}) async-start(s8[10485760]{0:T(1024)(128)(4,1)} %bitcast.273), calls=%async_computation.4 | async-start | bytes 8388608
  882.8 28.3 %slice-start.1 = ((s8[10485760]{0:T(1024)(128)(4,1)}), s8[4194304]{0:T(1024)(128)(4,1)S(1)}, s32[]{:S(2)}) async-start(s8[10485760]{0:T(1024)(128)(4,1)} %bitcast.273), calls=%async_computation.5 | async-start | bytes 8388608
  897.7 13.4 slice-start.2
  1007.5 14.4 %copy-start = (f32[1024,2048]{0,1:T(8,128)S(1)}, f32[1024,2048]{0,1:T(8,128)}, u32[]{:S(2)}) copy-start(f32[1024,2048]{0,1:T(8,128)} %fusion.100) | copy-start | bytes 25165828
  1021.8 15.9 %copy-start.7 = (f32[128,128]{1,0:T(8,128)S(1)}, f32[128,128]{1,0:T(8,128)}, u32[]{:S(2)}) copy-start(f32[128,128]{1,0:T(8,128)} %fusion.177) | copy-start | bytes 196612
  1038.3 3.3 copy-start.1
  1082.3 7.2 copy-start.3
  1093.0 216.8 %copy-start.4 = (f32[256,2048]{0,1:T(8,128)S(1)}, f32[256,2048]{0,1:T(8,128)}, u32[]{:S(2)}) copy-start(f32[256,2048]{0,1:T(8,128)} %copy.216) | copy-start | bytes 6291460
Sparse Core Ops, SparseCore 0:
  102.0 215.3 all-gather.2
  320.2 87.1 all-gather.4
  1089.6 220.1 all-reduce.3
where the time goes:
time: 1360 us; the launch traced here: 1350 us
  waiting for transfers between devices  479 us (35%)
  other arithmetic  415 us (31%)
  matrix products  331 us (24%)
  local copies, waits for them, and re-layouts  102 us (8%)
  between operations  15 us (1%)
    psum x1, waiting for transfers between devices, from_root(): return lax.psum(kept, axis)  211 us
    all_gather x1, waiting for transfers between devices, local(): pieces = lax.all_gather(corner, ('row', 'col'), axis=0, tiled=True)  209 us
    another operation x48, other arithmetic, block_cholesky(): diag_factor = jnp.linalg.cholesky(column[:BLK])  200 us
    another operation x32, other arithmetic, block_cholesky(): jax.scipy.linalg.solve_triangular(diag_factor, identity, lower=True)  178 us
    dot_general x15, matrix products, block_solve(): jnp.dot(result[:, :start], factor[start:start + BLK, :start].T, precision...  132 us
    dot_general x15, matrix products, block_cholesky(): jnp.dot(factor[start:, :start], factor[start:start + BLK, :start].T, prec...  77.6 us
    all_to_all x1, waiting for transfers between devices, local(): lax.all_to_all(outgoing, 'row', split_axis=1, concat_axis=1, tiled=True)  58.4 us
    dot_general x16, matrix products, block_solve(): jnp.dot(target, inverses[step].T, precision=lax.Precision.HIGHEST, prefer...  43.4 us
  transfers between devices with their start and end apart: 4, of which 3 were waited for; matrix products, arithmetic and copies ran while one was open for 40% of the time, Pallas kernels for 0%

commit v1 on v0

--- a/solution.py
+++ b/solution.py
@@ -9,7 +9,7 @@
 
 def from_root(value, axis, source):
     kept = jnp.where(lax.axis_index(axis) == source, value, 0).astype(value.dtype)
-    return lax.psum(kept, axis)
+    return lax.all_gather(kept, axis_name=axis).sum(axis=0)
 
 
 def block_cholesky(leading):

time: 1360 us -> 1970 us (1.45)
  waiting for transfers between devices: 479 us -> 1060 us
  matrix products: 331 us -> 355 us
    all_gather x0 -> x1, waiting for transfers between devices: none -> 789 us  [from_root(): return lax.all_gather(kept, axis_name=axis).sum(axis=0)]
    psum x1 -> x0, waiting for transfers between devices: 211 us -> none  [from_root(): return lax.psum(kept, axis)]
    dot_general x1, matrix products: 31.6 us -> 55 us  [local(): jnp.dot(factor_rows, column_rows.T, precision=lax.Precision.HIGHEST, pref...]
  transfers between devices with their start and end apart: 4 -> 4, of which waited for: 3 -> 3; matrix products, arithmetic and copies ran while one was open for 40% -> 28% of each run, Pallas kernels for 0% -> 0%
where the time goes in v1:
time: 1970 us; the launch traced here: 1960 us
  waiting for transfers between devices  1060 us (54%)
  other arithmetic  420 us (21%)
  matrix products  355 us (18%)
  local copies, waits for them, and re-layouts  106 us (5%)
    all_gather x1, waiting for transfers between devices, from_root(): return lax.all_gather(kept, axis_name=axis).sum(axis=0)  789 us
    all_gather x1, waiting for transfers between devices, local(): pieces = lax.all_gather(corner, ('row', 'col'), axis=0, tiled=True)  209 us
    another operation x48, other arithmetic, block_cholesky(): diag_factor = jnp.linalg.cholesky(column[:BLK])  200 us
    another operation x32, other arithmetic, block_cholesky(): jax.scipy.linalg.solve_triangular(diag_factor, identity, lower=True)  178 us
    dot_general x15, matrix products, block_solve(): jnp.dot(result[:, :start], factor[start:start + BLK, :start].T, precision...  132 us
    dot_general x15, matrix products, block_cholesky(): jnp.dot(factor[start:, :start], factor[start:start + BLK, :start].T, prec...  77.6 us
    all_to_all x1, waiting for transfers between devices, local(): lax.all_to_all(outgoing, 'row', split_axis=1, concat_axis=1, tiled=True)  58.4 us
    dot_general x1, matrix products, local(): jnp.dot(factor_rows, column_rows.T, precision=lax.Precision.HIGHEST, pref...  55 us
  transfers between devices with their start and end apart: 4, of which 3 were waited for; matrix products, arithmetic and copies ran while one was open for 28% of the time, Pallas kernels for 0%

profile of v1, /device:TPU:1, one launch (start us, length us, event | category | flops | bytes accessed | tf_op | source)
XLA Modules:
  0.0 1957.4 jit_solution(17670833727957370574)
XLA Ops:
  18.3 58.4 %all-to-all-done = f32[2,8,128,512]{3,2,0,1:T(8,128)} async-done(((f32[2,8,128,512]{3,2,0,1:T(8,128)}), f32[2,8,128,512]{3,2,0,1:T(8,128)}, u32[]{:S(2)}, u32[]{:S(2)}) %all-to-all-start) | async-done | bytes 4194336 | tf_op jit(solution)/shard_map/all_to_all | solution.py:83
  108.5 208.7 %all-gather.4.cloned.1.call-done = f32[32768,128]{1,0:T(8,128)} async-done(((f32[256,128]{1,0:T(8,128)}), f32[32768,128]{1,0:T(8,128)}) %all-gather.4.cloned.1.call-update) | async-done | bytes 16777232 | tf_op jit(solution)/shard_map/all_gather | solution.py:120
  317.3 17.8 copy.165
  335.0 18.0 reshape.1466
  354.8 11.7 cholesky.254
  367.8 9.8 custom-call.20
  392.1 11.9 cholesky.265
  405.9 9.8 custom-call.21
  422.5 11.7 cholesky.276
  436.2 10.0 custom-call.22
  453.9 11.7 cholesky.287
  467.6 9.8 custom-call.23
  486.1 11.7 cholesky.298
  499.8 9.8 custom-call.24
  518.2 11.7 cholesky.309
  531.9 9.8 custom-call.25
  550.9 11.7 cholesky.320
  564.6 9.8 custom-call.26
  583.4 12.1 cholesky.331
  597.5 9.8 custom-call.27
  616.5 11.9 cholesky.342
  630.3 9.8 custom-call.28
  648.6 11.9 cholesky.353
  662.4 9.8 custom-call.29
  680.7 11.7 cholesky.364
  694.4 10.2 custom-call.30
  712.3 11.7 cholesky.375
  725.9 9.8 custom-call.31
  743.1 11.7 cholesky.386
  756.8 9.8 custom-call.32
  772.7 11.9 cholesky.397
  786.6 9.8 custom-call.33
  801.6 11.7 cholesky.408
  815.3 10.2 custom-call.34
  829.4 11.7 cholesky.419
  849.8 9.8 custom-call.35
  934.0 9.7 fusion.118
  946.8 10.5 fusion.95
  960.4 11.5 fusion.121
  975.0 12.6 fusion.71
  990.6 13.4 fusion.74
  1007.1 14.3 fusion.124
  1022.9 14.6 fusion.77
  1047.8 13.3 reshape.1470
  1069.8 11.8 copy.201
  1089.2 788.9 %all-gather.8.cloned.1.call-done = f32[8,640,2048]{2,1,0:T(8,128)} async-done(((f32[1,640,2048]{2,1,0:T(8,128)}), f32[8,640,2048]{2,1,0:T(8,128)}) %all-gather.8.cloned.1.call-update) | async-done | bytes 41943056 | tf_op jit(solution)/shard_map/all_gather | solution.py:12
  1878.2 17.3 reduce_sum.29
  1895.4 55.0 %fusion.32 = f32[1280,640]{1,0:T(8,128)} fusion(f32[1280,640]{1,0:T(8,128)} %copy-done.5, f32[640,2048]{1,0:T(8,128)} %reduce_sum.29, pred[640]{0:T(1024)(128)(4,1)S(1)} %fusion.277, pred[1280]{0:T(1024)(128)(4,1)S(1)} %fusion.273, f32[1024,2048]{0,1:T(8,128)} %copy-done.1, f32[256,2048]{0,1:T(8,128)S(1)} %copy-done.4), kind=kOutput, calls=%fused_computation.37 | convolution fusion | flops 20137738240 | bytes 22284160 | tf_op jit(solution)/shard_map/dot_general | solution.py:138
  (237 shorter events, 320.1 us)
Async XLA Ops:
  7.2 10.9 copy-start.8
  11.9 64.8 %all-to-all-start = ((f32[2,8,128,512]{3,2,0,1:T(8,128)}), f32[2,8,128,512]{3,2,0,1:T(8,128)}, u32[]{:S(2)}, u32[]{:S(2)}) async-start(f32[2,8,128,512]{3,2,0,1:T(8,128)} %copy.160), calls=%async_computation | async-start | bytes 8388608 | tf_op jit(solution)/shard_map/all_to_all | solution.py:83
  17.8 299.5 %all-gather.4.cloned.1.call-start = ((), (), s32[]{:S(2)}) async-start(), calls=%async_computation.1 | async-start | bytes 16908288 | tf_op jit(solution)/shard_map/all_gather | solution.py:120
  89.3 9.9 copy-start.6
  101.0 234.0 %copy-start.5 = (f32[1280,640]{1,0:T(8,128)}, f32[1280,640]{1,0:T(8,128)S(1)}, u32[]{:S(2)}) copy-start(f32[1280,640]{1,0:T(8,128)S(1)} %bitcast_add_fusion) | copy-start | bytes 9830404
  101.8 741.5 %all-gather.6.cloned.1.call-start = ((), (), s32[]{:S(2)}) async-start(), calls=%async_computation.2 | async-start | bytes 11141120 | tf_op jit(solution)/shard_map/all_gather | solution.py:113
  108.5 1769.7 %all-gather.8.cloned.1.call-start = ((), (), s32[]{:S(2)}) async-start(), calls=%async_computation.3 | async-start | bytes 47185920 | tf_op jit(solution)/shard_map/all_gather | solution.py:12
  862.3 35.0 %copy-start.2 = (f32[2,1,128,2048]{3,2,1,0:T(8,128)}, f32[2,1,128,2048]{3,2,1,0:T(8,128)S(1)}, u32[]{:S(2)}) copy-start(f32[2,1,128,2048]{3,2,1,0:T(8,128)S(1)} %constant_dynamic-slice_fusion) | copy-start | bytes 6291460
  874.9 35.9 %slice-start = ((s8[10485760]{0:T(1024)(128)(4,1)}), s8[4194304]{0:T(1024)(128)(4,1)S(1)}, s32[]{:S(2)}) async-start(s8[10485760]{0:T(1024)(128)(4,1)} %bitcast.267), calls=%async_computation.4 | async-start | bytes 8388608
  882.4 28.4 %slice-start.1 = ((s8[10485760]{0:T(1024)(128)(4,1)}), s8[4194304]{0:T(1024)(128)(4,1)S(1)}, s32[]{:S(2)}) async-start(s8[10485760]{0:T(1024)(128)(4,1)} %bitcast.267), calls=%async_computation.5 | async-start | bytes 8388608
  897.3 13.5 slice-start.2
  1007.1 14.4 copy-start
  1021.5 16.0 copy-start.7
  1038.1 3.2 copy-start.1
  1069.8 11.8 copy-start.3
  1089.2 806.2 %copy-start.4 = (f32[256,2048]{0,1:T(8,128)S(1)}, f32[256,2048]{0,1:T(8,128)}, u32[]{:S(2)}) copy-start(f32[256,2048]{0,1:T(8,128)} %copy.222) | copy-start | bytes 6291460
Sparse Core Ops, SparseCore 0:
  101.9 215.3 all-gather.3
  320.1 87.2 all-gather.5
  1081.7 796.4 all-gather.7
